TPU v7x, 512 devices: a whole 4x4x16 slice. The times are simulated.
512 devices in a mesh: head: 8 (over z_hi, x), ctx: 64 (over z_lo, y, core).
Axes of the slice: x: 4, y: 4, z: 16 (z_hi: 2, z_lo: 8; z = z_hi * 8 + z_lo), core: 2. Of those that a mesh axis runs over, the one named last changes fastest.
Arguments:
- queries: bfloat16 [128, 128, 8192], P('ctx', 'head'), may hold values from -4 to 4
- keys: bfloat16 [128, 128, 1024], P('ctx', 'head'), may hold values from -32 to 32
- values: bfloat16 [128, 128, 1024], P('ctx', 'head'), may hold values from -6 to 6
- doc_ids: int32 [128], replicated, may hold values from 0 to 15, never falling along the last dimension, each value on 1 to 65 neighbouring positions
Outputs:
- attended: bfloat16 [128, 128, 8192], P('ctx', 'head')
Inputs may be any that keep to these rules, and one draw needn't show every extreme that they name: `doc_ids`: ids never fall along the blocks; every document covers 1 to 65 whole blocks, one of them exactly 65.
All inputs are finite; a program needn't handle non-finite values.
Results may differ from a plain program's by a relative error of at most 0.0045.
Values may be sent and summed in bfloat16 or wider, within the bound.
A program may use at most 64 MiB of HBM per device.

v0:
```python
import math

import jax
import jax.numpy as jnp
from jax import lax
from jax.sharding import PartitionSpec as P

HD = 128
GROUP = 8
BLK = 128


def attend(state, query_rows, query_pos, query_first, piece, start_block):
    key_count = piece.shape[1] * piece.shape[2]
    heads_kv = piece.shape[3] // HD
    key_pos = start_block * BLK + jnp.arange(key_count, dtype=jnp.int32)
    needed = (key_pos[0] <= jnp.max(query_pos)) & (key_pos[key_count - 1] >= jnp.min(query_first))

    def compute(current):
        best, totals, sums = current
        key_rows = piece[0].reshape(key_count, heads_kv, HD)
        value_rows = piece[1].reshape(key_count, heads_kv, HD)
        scores = jnp.einsum(
            "rkgd,tkd->rkgt", query_rows, key_rows, preferred_element_type=jnp.float32
        ) * HD ** (-0.5)
        allowed = (key_pos[None, :] <= query_pos[:, None]) & (
            key_pos[None, :] >= query_first[:, None]
        )
        allowed = allowed[:, None, None, :]
        fresh = jnp.maximum(best, jnp.max(jnp.where(allowed, scores, -1e30), axis=-1))
        weights = jnp.where(allowed, jnp.exp(scores - fresh[..., None]), 0.0)
        factor = jnp.exp(best - fresh)
        totals = totals * factor + jnp.sum(weights, axis=-1)
        mixed = jnp.einsum(
            "rkgt,tkd->rkgd",
            weights.astype(jnp.bfloat16),
            value_rows,
            preferred_element_type=jnp.float32,
        )
        return (fresh, totals, sums * factor[..., None] + mixed)

    return lax.cond(needed, compute, lambda current: current, state)


def attend_blocks(state, query_rows, query_pos, query_first, piece):
    block_count = piece.shape[1]
    group_size = math.gcd(block_count, max(1, 512 // BLK))

    def one_group(index, current):
        part_piece = lax.dynamic_slice_in_dim(piece, index * group_size, group_size, 1)
        return attend(current, query_rows, query_pos, query_first, part_piece, index * group_size)

    return lax.fori_loop(0, block_count // group_size, one_group, state)


def on_device(queries, keys, values, doc_ids):
    moved_q, moved_k, moved_v = (
        lax.all_to_all(queries, "head", split_axis=2, concat_axis=1, tiled=True),
        lax.all_to_all(keys, "head", split_axis=2, concat_axis=1, tiled=True),
        lax.all_to_all(values, "head", split_axis=2, concat_axis=1, tiled=True),
    )
    own_blocks = moved_q.shape[0]
    rows = own_blocks * BLK
    heads_kv = moved_k.shape[2] // HD
    here = lax.axis_index("ctx")
    first_block = jnp.sum((doc_ids[None, :] < doc_ids[:, None]).astype(jnp.int32), axis=1)
    query_rows = moved_q.reshape(rows, heads_kv, GROUP, HD)
    chain = jnp.stack([moved_k, moved_v])
    positions = here * rows + jnp.arange(rows, dtype=jnp.int32)
    firsts = (
        jnp.repeat(lax.dynamic_slice_in_dim(first_block, here * own_blocks, own_blocks), BLK) * BLK
    )
    tasks = [(query_rows,) + (positions, firsts)]
    states = tuple(
        (
            (
                jnp.full((rows, heads_kv, task[0].shape[2]), -1e30, jnp.float32),
                jnp.zeros((rows, heads_kv, task[0].shape[2]), jnp.float32),
                jnp.zeros((rows, heads_kv, task[0].shape[2], HD), jnp.float32),
            )
            for task in tasks
        )
    )
    piece = lax.all_gather(chain, "ctx", axis=1, tiled=True)
    states = tuple(
        (
            attend_blocks(states[number], task[0], task[1], task[2], piece)
            for number, task in enumerate(tasks)
        )
    )
    finished = [(state[2] / state[1][..., None]).astype(jnp.bfloat16) for state in states]
    whole = finished[0]
    whole = whole.reshape(own_blocks, BLK, heads_kv * GROUP * HD)
    return lax.all_to_all(whole, "head", split_axis=1, concat_axis=2, tiled=True)


def solution(mesh):
    in_specs = (P("ctx", "head", None), P("ctx", "head", None), P("ctx", "head", None), P())
    out_specs = P("ctx", "head", None)
    return jax.shard_map(
        on_device, mesh=mesh, in_specs=in_specs, out_specs=out_specs, check_vma=False
    )
```

profile of v0, /device:TPU:224, one launch (start us, length us, event | category | flops | bytes accessed | tf_op | source)
XLA Modules:
  0.0 405.5 jit_solution(5322700162328578628)
XLA Ops:
  8.9 10.0 %all-to-all-start = ((bf16[8,2,2048]{2,1,0:T(2,128)(2,1)}), bf16[8,2,2048]{2,1,0:T(2,128)(2,1)S(1)}, u32[]{:S(2)}, u32[]{:S(2)}) async-start(bf16[8,2,2048]{2,1,0:T(2,128)(2,1)} %reshape.118), calls=%async_computation | async-start | bytes 131072 | tf_op jit(solution)/shard_map/all_to_all | solution.py:59
  21.2 12.8 %all-to-all-done = bf16[8,2,2048]{2,1,0:T(2,128)(2,1)S(1)} async-done(((bf16[8,2,2048]{2,1,0:T(2,128)(2,1)}), bf16[8,2,2048]{2,1,0:T(2,128)(2,1)S(1)}, u32[]{:S(2)}, u32[]{:S(2)}) %all-to-all-start) | async-done | bytes 65568 | tf_op jit(solution)/shard_map/all_to_all | solution.py:59
  38.1 14.2 %all-to-all-done.1 = bf16[8,2,2048]{2,1,0:T(2,128)(2,1)S(1)} async-done(((bf16[8,2,2048]{2,1,0:T(2,128)(2,1)}), bf16[8,2,2048]{2,1,0:T(2,128)(2,1)S(1)}, u32[]{:S(2)}, u32[]{:S(2)}) %all-to-all-start.1) | async-done | bytes 65568 | tf_op jit(solution)/shard_map/all_to_all | solution.py:60
  53.8 6.8 %copy.54 = bf16[2,16,8192]{1,0,2:T(2,128)(2,1)} copy(bf16[2,16,8192]{2,1,0:T(8,128)(2,1)S(1)} %copy-done) | data formatting | bytes 1048576 | tf_op args[0]
  60.6 6.5 %reshape.120 = bf16[8,2,16384]{2,1,0:T(2,128)(2,1)} reshape(bf16[8192,2,16]{2,1,0:T(2,128)(2,1)} %bitcast.100) | data formatting | bytes 1048576
  72.2 33.1 %all-to-all-done.2 = bf16[8,2,16384]{2,1,0:T(2,128)(2,1)S(1)} async-done(((bf16[8,2,16384]{2,1,0:T(2,128)(2,1)}), bf16[8,2,16384]{2,1,0:T(2,128)(2,1)S(1)}, u32[]{:S(2)}, u32[]{:S(2)}) %all-to-all-start.2) | async-done | bytes 524320 | tf_op jit(solution)/shard_map/all_to_all | solution.py:58
  105.3 4.1 %reshape.121 = bf16[8192,2,16]{2,1,0:T(2,128)(2,1)} reshape(bf16[8,2,16384]{2,1,0:T(2,128)(2,1)S(1)} %all-to-all-done.2) | data formatting | bytes 1048576
  109.4 8.9 %copy.55 = bf16[2,16,8,1024]{3,1,2,0:T(8,128)(2,1)S(1)} copy(bf16[2,16,8,1024]{1,0,3,2:T(2,128)(2,1)} %bitcast.99) | data formatting | bytes 1048576 | tf_op jit(solution)/shard_map/all_to_all | solution.py:58
  118.5 76.7 %all-gather.2.cloned.1.call-done = bf16[2,128,128,128]{3,2,1,0:T(8,128)(2,1)} async-done(((bf16[2,2,128,128]{3,2,1,0:T(8,128)(2,1)}), bf16[2,128,128,128]{3,2,1,0:T(8,128)(2,1)}) %all-gather.2.cloned.1.call-update) | async-done | bytes 8388624 | tf_op jit(solution)/shard_map/all_gather | solution.py:84
  195.3 173.9 %while.20 = (s32[]{:T(128)}, f32[256,1,8]{0,2,1:T(8,128)S(1)}, f32[256,1,8]{0,2,1:T(8,128)S(1)}, f32[256,1,8,128]{0,3,2,1:T(8,128)S(1)}, s32[]{:T(128)}, /*index...) while((s32[]{:T(128)}, f32[256,1,8]{0,2,1:T(8,128)S(1)}, ...), condition=%wide.region_8.9_spmd.clone, body=%wide.region_3.8_spmd.clone.sunk | while | flops 549329664 | bytes 16656773 | solution.py:53
  237.6 4.1 %conditional.3 = ((f32[256,1,8]{0,2,1:T(8,128)S(1)}, f32[256,1,8]{0,2,1:T(8,128)S(1)}, f32[256,1,8,128]{0,3,2,1:T(8,128)S(1)})) conditional(s32[]{:T(128)} %convert_element_type.35, (f32[256,1,8]{0,2,1:T(8,128)S(1)}, f32[256,1,8]{0,2,1:T(8,128)S(1)}, f32[256,1,8,128]{0,3,2,1:T(8,128)S(1)}) %tuple.73, (s32[512]{0:T(512)S(1)}, s32[]{:T(128)}, ...), branch_computations={%region_4.0_spmd, %region_5.7_spmd} | conditional | flops 549329152 | bytes 16652390 | solution.py:42
  244.9 4.1 %conditional.3 = ((f32[256,1,8]{0,2,1:T(8,128)S(1)}, f32[256,1,8]{0,2,1:T(8,128)S(1)}, f32[256,1,8,128]{0,3,2,1:T(8,128)S(1)})) conditional(s32[]{:T(128)} %convert_element_type.35, (f32[256,1,8]{0,2,1:T(8,128)S(1)}, f32[256,1,8]{0,2,1:T(8,128)S(1)}, f32[256,1,8,128]{0,3,2,1:T(8,128)S(1)}) %tuple.73, (s32[512]{0:T(512)S(1)}, s32[]{:T(128)}, ...), branch_computations={%region_4.0_spmd, %region_5.7_spmd} | conditional | flops 549329152 | bytes 16652390 | solution.py:42
  252.3 4.1 %conditional.3 = ((f32[256,1,8]{0,2,1:T(8,128)S(1)}, f32[256,1,8]{0,2,1:T(8,128)S(1)}, f32[256,1,8,128]{0,3,2,1:T(8,128)S(1)})) conditional(s32[]{:T(128)} %convert_element_type.35, (f32[256,1,8]{0,2,1:T(8,128)S(1)}, f32[256,1,8]{0,2,1:T(8,128)S(1)}, f32[256,1,8,128]{0,3,2,1:T(8,128)S(1)}) %tuple.73, (s32[512]{0:T(512)S(1)}, s32[]{:T(128)}, ...), branch_computations={%region_4.0_spmd, %region_5.7_spmd} | conditional | flops 549329152 | bytes 16652390 | solution.py:42
  259.7 4.1 %conditional.3 = ((f32[256,1,8]{0,2,1:T(8,128)S(1)}, f32[256,1,8]{0,2,1:T(8,128)S(1)}, f32[256,1,8,128]{0,3,2,1:T(8,128)S(1)})) conditional(s32[]{:T(128)} %convert_element_type.35, (f32[256,1,8]{0,2,1:T(8,128)S(1)}, f32[256,1,8]{0,2,1:T(8,128)S(1)}, f32[256,1,8,128]{0,3,2,1:T(8,128)S(1)}) %tuple.73, (s32[512]{0:T(512)S(1)}, s32[]{:T(128)}, ...), branch_computations={%region_4.0_spmd, %region_5.7_spmd} | conditional | flops 549329152 | bytes 16652390 | solution.py:42
  267.0 4.1 %conditional.3 = ((f32[256,1,8]{0,2,1:T(8,128)S(1)}, f32[256,1,8]{0,2,1:T(8,128)S(1)}, f32[256,1,8,128]{0,3,2,1:T(8,128)S(1)})) conditional(s32[]{:T(128)} %convert_element_type.35, (f32[256,1,8]{0,2,1:T(8,128)S(1)}, f32[256,1,8]{0,2,1:T(8,128)S(1)}, f32[256,1,8,128]{0,3,2,1:T(8,128)S(1)}) %tuple.73, (s32[512]{0:T(512)S(1)}, s32[]{:T(128)}, ...), branch_computations={%region_4.0_spmd, %region_5.7_spmd} | conditional | flops 549329152 | bytes 16652390 | solution.py:42
  274.4 4.1 %conditional.3 = ((f32[256,1,8]{0,2,1:T(8,128)S(1)}, f32[256,1,8]{0,2,1:T(8,128)S(1)}, f32[256,1,8,128]{0,3,2,1:T(8,128)S(1)})) conditional(s32[]{:T(128)} %convert_element_type.35, (f32[256,1,8]{0,2,1:T(8,128)S(1)}, f32[256,1,8]{0,2,1:T(8,128)S(1)}, f32[256,1,8,128]{0,3,2,1:T(8,128)S(1)}) %tuple.73, (s32[512]{0:T(512)S(1)}, s32[]{:T(128)}, ...), branch_computations={%region_4.0_spmd, %region_5.7_spmd} | conditional | flops 549329152 | bytes 16652390 | solution.py:42
  281.7 4.1 %conditional.3 = ((f32[256,1,8]{0,2,1:T(8,128)S(1)}, f32[256,1,8]{0,2,1:T(8,128)S(1)}, f32[256,1,8,128]{0,3,2,1:T(8,128)S(1)})) conditional(s32[]{:T(128)} %convert_element_type.35, (f32[256,1,8]{0,2,1:T(8,128)S(1)}, f32[256,1,8]{0,2,1:T(8,128)S(1)}, f32[256,1,8,128]{0,3,2,1:T(8,128)S(1)}) %tuple.73, (s32[512]{0:T(512)S(1)}, s32[]{:T(128)}, ...), branch_computations={%region_4.0_spmd, %region_5.7_spmd} | conditional | flops 549329152 | bytes 16652390 | solution.py:42
  289.1 4.1 %conditional.3 = ((f32[256,1,8]{0,2,1:T(8,128)S(1)}, f32[256,1,8]{0,2,1:T(8,128)S(1)}, f32[256,1,8,128]{0,3,2,1:T(8,128)S(1)})) conditional(s32[]{:T(128)} %convert_element_type.35, (f32[256,1,8]{0,2,1:T(8,128)S(1)}, f32[256,1,8]{0,2,1:T(8,128)S(1)}, f32[256,1,8,128]{0,3,2,1:T(8,128)S(1)}) %tuple.73, (s32[512]{0:T(512)S(1)}, s32[]{:T(128)}, ...), branch_computations={%region_4.0_spmd, %region_5.7_spmd} | conditional | flops 549329152 | bytes 16652390 | solution.py:42
  296.5 4.1 %conditional.3 = ((f32[256,1,8]{0,2,1:T(8,128)S(1)}, f32[256,1,8]{0,2,1:T(8,128)S(1)}, f32[256,1,8,128]{0,3,2,1:T(8,128)S(1)})) conditional(s32[]{:T(128)} %convert_element_type.35, (f32[256,1,8]{0,2,1:T(8,128)S(1)}, f32[256,1,8]{0,2,1:T(8,128)S(1)}, f32[256,1,8,128]{0,3,2,1:T(8,128)S(1)}) %tuple.73, (s32[512]{0:T(512)S(1)}, s32[]{:T(128)}, ...), branch_computations={%region_4.0_spmd, %region_5.7_spmd} | conditional | flops 549329152 | bytes 16652390 | solution.py:42
  303.8 4.1 %conditional.3 = ((f32[256,1,8]{0,2,1:T(8,128)S(1)}, f32[256,1,8]{0,2,1:T(8,128)S(1)}, f32[256,1,8,128]{0,3,2,1:T(8,128)S(1)})) conditional(s32[]{:T(128)} %convert_element_type.35, (f32[256,1,8]{0,2,1:T(8,128)S(1)}, f32[256,1,8]{0,2,1:T(8,128)S(1)}, f32[256,1,8,128]{0,3,2,1:T(8,128)S(1)}) %tuple.73, (s32[512]{0:T(512)S(1)}, s32[]{:T(128)}, ...), branch_computations={%region_4.0_spmd, %region_5.7_spmd} | conditional | flops 549329152 | bytes 16652390 | solution.py:42
  311.2 4.1 %conditional.3 = ((f32[256,1,8]{0,2,1:T(8,128)S(1)}, f32[256,1,8]{0,2,1:T(8,128)S(1)}, f32[256,1,8,128]{0,3,2,1:T(8,128)S(1)})) conditional(s32[]{:T(128)} %convert_element_type.35, (f32[256,1,8]{0,2,1:T(8,128)S(1)}, f32[256,1,8]{0,2,1:T(8,128)S(1)}, f32[256,1,8,128]{0,3,2,1:T(8,128)S(1)}) %tuple.73, (s32[512]{0:T(512)S(1)}, s32[]{:T(128)}, ...), branch_computations={%region_4.0_spmd, %region_5.7_spmd} | conditional | flops 549329152 | bytes 16652390 | solution.py:42
  318.5 4.1 %conditional.3 = ((f32[256,1,8]{0,2,1:T(8,128)S(1)}, f32[256,1,8]{0,2,1:T(8,128)S(1)}, f32[256,1,8,128]{0,3,2,1:T(8,128)S(1)})) conditional(s32[]{:T(128)} %convert_element_type.35, (f32[256,1,8]{0,2,1:T(8,128)S(1)}, f32[256,1,8]{0,2,1:T(8,128)S(1)}, f32[256,1,8,128]{0,3,2,1:T(8,128)S(1)}) %tuple.73, (s32[512]{0:T(512)S(1)}, s32[]{:T(128)}, ...), branch_computations={%region_4.0_spmd, %region_5.7_spmd} | conditional | flops 549329152 | bytes 16652390 | solution.py:42
  325.9 4.1 %conditional.3 = ((f32[256,1,8]{0,2,1:T(8,128)S(1)}, f32[256,1,8]{0,2,1:T(8,128)S(1)}, f32[256,1,8,128]{0,3,2,1:T(8,128)S(1)})) conditional(s32[]{:T(128)} %convert_element_type.35, (f32[256,1,8]{0,2,1:T(8,128)S(1)}, f32[256,1,8]{0,2,1:T(8,128)S(1)}, f32[256,1,8,128]{0,3,2,1:T(8,128)S(1)}) %tuple.73, (s32[512]{0:T(512)S(1)}, s32[]{:T(128)}, ...), branch_computations={%region_4.0_spmd, %region_5.7_spmd} | conditional | flops 549329152 | bytes 16652390 | solution.py:42
  371.0 26.6 %all_to_all.63 = bf16[2,128,1024]{2,0,1:T(2,128)(2,1)S(1)} all-to-all(bf16[2,128,1024]{2,0,1:T(2,128)(2,1)S(1)} %copy.58), channel_id=1, replica_groups=mesh['head'=8,'ctx'=64] {'head'}, dimensions={1} | all-to-all | bytes 1048576 | tf_op jit(solution)/shard_map/all_to_all | solution.py:94
  (331 shorter events, 124.5 us)
Async XLA Ops:
  6.5 47.2 %copy-start = (bf16[2,16,8192]{2,1,0:T(8,128)(2,1)S(1)}, bf16[2,16,8192]{2,1,0:T(8,128)(2,1)}, u32[]{:S(2)}) copy-start(bf16[2,16,8192]{2,1,0:T(8,128)(2,1)} %param.8) | copy-start | bytes 1572868
  8.9 25.1 %all-to-all-start = ((bf16[8,2,2048]{2,1,0:T(2,128)(2,1)}), bf16[8,2,2048]{2,1,0:T(2,128)(2,1)S(1)}, u32[]{:S(2)}, u32[]{:S(2)}) async-start(bf16[8,2,2048]{2,1,0:T(2,128)(2,1)} %reshape.118), calls=%async_computation | async-start | bytes 131072 | tf_op jit(solution)/shard_map/all_to_all | solution.py:59
  34.0 18.4 %all-to-all-start.1 = ((bf16[8,2,2048]{2,1,0:T(2,128)(2,1)}), bf16[8,2,2048]{2,1,0:T(2,128)(2,1)S(1)}, u32[]{:S(2)}, u32[]{:S(2)}) async-start(bf16[8,2,2048]{2,1,0:T(2,128)(2,1)} %reshape.116), calls=%async_computation.1 | async-start | bytes 131072 | tf_op jit(solution)/shard_map/all_to_all | solution.py:60
  37.4 157.8 %all-gather.2.cloned.1.call-start = ((), (), s32[]{:S(2)}) async-start(), calls=%async_computation.4 | async-start | bytes 8519680 | tf_op jit(solution)/shard_map/all_gather | solution.py:84
  53.8 17.4 %copy-start.1 = (s32[128]{0:T(128)S(1)}, s32[128]{0:T(128)}, u32[]{:S(2)}) copy-start(s32[128]{0:T(128)} %param.11) | copy-start | bytes 1540
  67.0 38.3 %all-to-all-start.2 = ((bf16[8,2,16384]{2,1,0:T(2,128)(2,1)}), bf16[8,2,16384]{2,1,0:T(2,128)(2,1)S(1)}, u32[]{:S(2)}, u32[]{:S(2)}) async-start(bf16[8,2,16384]{2,1,0:T(2,128)(2,1)} %reshape.120), calls=%async_computation.2 | async-start | bytes 1048576 | tf_op jit(solution)/shard_map/all_to_all | solution.py:58
Sparse Core Ops, SparseCore 0:
  53.9 141.2 all-gather.1
where the time goes:
time: 408 us; the launch traced here: 405 us
  waiting for transfers between devices  137 us (34%)
  loops' own time  84.3 us (21%)
  local copies, waits for them, and re-layouts  73.1 us (18%)
  matrix products  33.6 us (8%)
  blocking collectives  26.6 us (7%)
  other arithmetic  20.5 us (5%)
  starting transfers between devices  16.9 us (4%)
  between operations  13.6 us (3%)
    another operation x1, loops' own time, attend_blocks(): return lax.fori_loop(0, block_count // group_size, one_group, state)  82.7 us
    all_gather x1, waiting for transfers between devices, on_device(): piece = lax.all_gather(chain, 'ctx', axis=1, tiled=True)  76.7 us
    all_to_all x1, waiting for transfers between devices, on_device(): lax.all_to_all(queries, 'head', split_axis=2, concat_axis=1, tiled=True)  33.1 us
    all_to_all x1, blocking collectives, on_device(): lax.all_to_all(whole, 'head', split_axis=1, concat_axis=2, tiled=True)  26.6 us
    unnamed x15, local copies, waits for them, and re-layouts  22.9 us
    dot_general x17, matrix products, compute(): jnp.einsum('rkgt,tkd->rkgd', weights.astype(jnp.bfloat16), value_rows, pr...  20.1 us
    slice x32, local copies, waits for them, and re-layouts, attend(): key_pos[key_count - 1] >= jnp.min(query_first)  18.7 us
    slice x17, local copies, waits for them, and re-layouts, compute(): value_rows = piece[1].reshape(key_count, heads_kv, HD)  16.9 us
  transfers between devices with their start and end apart: 4, of which 4 were waited for; matrix products, arithmetic and copies ran while one was open for 8% of the time, Pallas kernels for 0%

commit v1 on v0

v1 whole, which is shorter than its diff:
```python
import jax
import jax.numpy as jnp
from jax import lax
from jax.experimental import pallas as pl
from jax.experimental.pallas import tpu as pltpu
from jax.sharding import PartitionSpec as P

HD = 128
GROUP = 8
BLK = 128
HALF = 64
COLS = GROUP * HD
NX, NZ, NLO = 4, 16, 8

BACK = (0, 1, 2, 3, 4, 4, 3, 2, 1, 0)
SLICES = len(BACK)
UP = {0: 1, 1: 2, 2: 3, 3: 5}
DOWN = {4: 6, 6: 7, 7: 8, 8: 9}
FAR = 4
KEYS = 16 * HALF
ROWS = GROUP * HALF
BIG = -1e30
SCALE = HD**-0.5 * 1.4426950408889634
MESH = pl.DeviceIdType.MESH

AT = {2: -1, 3: 4, 4: 6, 5: 8, 6: 10, 7: 14, 8: 18, 9: 22}
ACROSS = {1: 2, 2: 6, 3: 10, 4: 14, 5: 18, 6: 22, 7: 26, 8: 30, 9: 34}
TILES = 2


def kernel(
    doc_ref, q_ref, k_ref, v_ref, out_ref,
    kbuf, vbuf, q_in, qaug, kaug, vaug, acc, top, o_out,
    in_send, in_recv, hop_send, hop_recv, out_send, out_recv,
):
    head, ctx = lax.axis_index("head"), lax.axis_index("ctx")
    x, zhi = lax.rem(head, NX), lax.div(head, NX)
    lo, y, c = lax.div(ctx, 8), lax.rem(lax.div(ctx, 2), 4), lax.rem(ctx, 2)
    z = zhi * NLO + lo
    yh, ys = lax.div(y, 2), lax.rem(y, 2)

    def device(x, y, z, c):
        return (lax.div(z, NLO) * NX + x, lax.rem(z, NLO) * 8 + y * 2 + c)

    def turn(v, by, n):
        return lax.rem(v + by + n, n)

    def side(y):
        return lax.rem(lax.div(y + 1, 2), 2)

    y_pair = yh * 2 + 1 - ys
    y_same = 3 - y
    own, other = yh * 2 + c, (1 - yh) * 2 + c
    my_head = 2 * x + side(y)
    sibling = device(x, y, z, 1 - c)
    across = device(x, y_same, z, c)
    above = device(x, y, turn(z, 1, NZ), c)
    below = device(x, y, turn(z, -1, NZ), c)
    far_below = device(x, y, turn(z, -4, NZ), c)
    far_above = device(x, y, turn(z, 4, NZ), c)
    partners = [(dx, dy) for dx in range(NX) for dy in range(2)]

    barrier = pltpu.get_barrier_semaphore()
    greeted = [device(turn(x, dx, NX), (y, y_pair)[dy], z, c) for dx, dy in partners[1:]]
    greeted += [above, below, far_above, sibling, across]
    for one in greeted:
        pl.semaphore_signal(barrier, inc=1, device_id=one, device_id_type=MESH)
    pl.semaphore_wait(barrier, len(greeted))

    here = pl.ds(pl.multiple_of(x * 16, 16), 16)

    def inward(which, i):
        dx, dy = partners[i]
        xd, yd = turn(x, dx, NX), (y, y_pair)[dy]
        h = 2 * xd + side(yd)
        if which == 2:
            src = q_ref.at[:, :, pl.ds(pl.multiple_of(h * COLS, COLS), COLS)]
            dst = q_in.at[pl.ds(ys * 2, 2), here, :]
        else:
            src = (k_ref, v_ref)[which].at[:, :, pl.ds(pl.multiple_of(h * HD, HD), HD)]
            dst = (kbuf, vbuf)[which].at[0, own, pl.ds(ys * 2, 2), here, :]
        if i == 0:
            return pltpu.make_async_copy(src, dst, in_recv.at[which, 0])
        return pltpu.make_async_remote_copy(
            src_ref=src, dst_ref=dst, send_sem=in_send.at[which, i], recv_sem=in_recv.at[which, i],
            device_id=device(xd, yd, z, c), device_id_type=MESH,
        )

    def arrived(which):
        for i in range(len(partners)):
            copy = inward(which, i)
            copy.wait() if i == 0 else copy.wait_recv()

    for which in range(3):
        for i in range(len(partners)):
            inward(which, i).start()

    def hop(which, p, way):
        buf = (kbuf, vbuf)[which]
        src, dst_p, slot = own, p, 0
        if way == 0:
            dst_p, to = (UP[p], above) if p in UP else (DOWN[p], below)
        elif way == 1:
            to, slot = across, 1
        elif way == 2:
            to, slot = sibling, 2
        elif way == 3:
            src, to, slot = other, sibling, 3
        else:
            dst_p, to = FAR, far_below
        return pltpu.make_async_remote_copy(
            src_ref=buf.at[p, src], dst_ref=buf.at[dst_p, src],
            send_sem=hop_send.at[which, p, way], recv_sem=hop_recv.at[which, dst_p, slot],
            device_id=to, device_id_type=MESH,
        )

    def landed(which, p, slot):
        buf = (kbuf, vbuf)[which]
        pltpu.make_async_remote_copy(
            src_ref=buf.at[p, own], dst_ref=buf.at[p, own],
            send_sem=hop_send.at[which, p, 1], recv_sem=hop_recv.at[which, p, slot],
            device_id=across, device_id_type=MESH,
        ).wait_recv()

    def ways(p):
        return ([0] if p in UP or p in DOWN else []) + ([4] if p == 0 else []) + [1, 2]

    def forward(p):
        for which in range(2):
            if p == 0:
                arrived(which)
            else:
                landed(which, p, 0)
            for way in ways(p):
                hop(which, p, way).start()

    def cross(p):
        for which in range(2):
            landed(which, p, 1)
            hop(which, p, 3).start()

    def ready(p):
        for which in range(2):
            landed(which, p, 2)
            landed(which, p, 3)

    lane = lax.broadcasted_iota(jnp.int32, (1, HD), 1)
    row_of = lax.rem(lax.broadcasted_iota(jnp.int32, (ROWS, HD), 0), HALF)
    lanes = lax.broadcasted_iota(jnp.int32, (ROWS, HD), 1)
    for q in range(4):
        pick = (lanes == q) | (lanes == row_of + HALF)
        qaug[q, :, HD:] = jnp.where(pick, 1.0, 0.0).astype(jnp.bfloat16)
    vaug[:, HD:] = jnp.ones((KEYS, HD), jnp.bfloat16)
    for q in range(4):
        acc[q] = jnp.zeros((ROWS, 2 * HD), jnp.float32)
        top[q] = jnp.full((ROWS, HD), BIG, jnp.float32)

    forward(0)
    forward(1)
    cross(0)
    arrived(2)
    for q in range(4):
        for g in range(GROUP):
            qaug[q, pl.ds(g * HALF, HALF), :HD] = q_in[q, :, pl.ds(g * HD, HD)]
    for p, u in AT.items():
        if u < 0:
            forward(p)

    def prepare(p):
        kaug[:, :HD] = kbuf[p].reshape(KEYS, HD)
        vaug[:, :HD] = vbuf[p].reshape(KEYS, HD)
        back = jnp.int32(0)
        for at, by in enumerate(BACK):
            back = jnp.where(p == at, by, back)
        alike = (p == 0) | (zhi == 1)
        query_blocks = [lo * 16 + (yh * 2 + q // 2) * 4 + c * 2 + q % 2 for q in range(4)]
        query_docs = [doc_ref[b] for b in query_blocks]
        for i in range(16):
            block = (lo - back) * 16 + (i // 8 * 2 + i // 2 % 2) * 4 + i // 4 % 2 * 2 + i % 2
            doc = doc_ref[jnp.maximum(block, 0)]
            mask = jnp.zeros((1, HD), jnp.float32)
            for q in range(4):
                seen = (block < query_blocks[q]) | ((block == query_blocks[q]) & alike)
                seen = seen & (block >= 0) & (doc == query_docs[q])
                mask = jnp.where(lane == q, jnp.where(seen, 0.0, BIG), mask)
            kaug[pl.ds(i * HALF, HALF), HD:] = jnp.broadcast_to(mask, (HALF, HD)).astype(jnp.bfloat16)

    def triangle(q):
        tile_lane = lax.broadcasted_iota(jnp.int32, (HALF, HD), 1)
        tile_row = lax.broadcasted_iota(jnp.int32, (HALF, HD), 0)

        @pl.when(q > 0)
        def _():
            at = pl.ds(pl.multiple_of(own * 4 * HALF + (q - 1) * HALF, HALF), HALF)
            old = kaug[at, HD:].astype(jnp.float32)
            kaug[at, HD:] = jnp.where(tile_lane >= HALF, 0.0, old).astype(jnp.bfloat16)

        at = pl.ds(pl.multiple_of(own * 4 * HALF + q * HALF, HALF), HALF)
        old = kaug[at, HD:].astype(jnp.float32)
        hidden = tile_row > tile_lane - HALF
        new = jnp.where(tile_lane >= HALF, jnp.where(hidden, BIG, 0.0), old)
        kaug[at, HD:] = new.astype(jnp.bfloat16)

    def outward(dx, t):
        xd, yd = turn(x, dx, NX), yh * 2 + t
        src = o_out.at[pl.ds(t * 2, 2), pl.ds(pl.multiple_of(xd * 16, 16), 16), :]
        dst = out_ref.at[:, :, pl.ds(pl.multiple_of(my_head * COLS, COLS), COLS)]
        sem = out_recv.at[dx * 2 + ys]
        local = pltpu.make_async_copy(src, dst, sem)
        remote = pltpu.make_async_remote_copy(
            src_ref=src, dst_ref=dst, send_sem=out_send.at[dx * 2 + t], recv_sem=sem,
            device_id=device(xd, yd, z, c), device_id_type=MESH,
        )
        return local, remote

    def send_out(t):
        for dx in (2, 1, 3, 0):
            local, remote = outward(dx, t)
            if dx:
                remote.start()
            else:
                pl.when(ys == t)(local.start)
                pl.when(ys != t)(remote.start)

    events = {}
    for p in range(1, SLICES):
        if AT.get(p, -1) >= 0:
            events.setdefault(AT[p], []).append((forward, p))
        events.setdefault(ACROSS[p], []).append((cross, p))
    for p in range(SLICES):
        events.setdefault(p * 4, []).append((ready, p))
    events.setdefault(4 * SLICES - 2, []).append((send_out, 0))

    def unit(u, _):
        p, q = lax.div(u, 4), lax.rem(u, 4)
        for when, what in sorted(events.items()):

            @pl.when(u == when)
            def _(what=what):
                for act, arg in what:
                    act(arg)

        pl.when(q == 0)(lambda: prepare(p))
        pl.when(p == 0)(lambda: triangle(q))

        span = ROWS // TILES
        for r in range(TILES):
            rows = pl.ds(r * span, span)
            scores = lax.dot_general(
                qaug[q, rows, :], kaug[...], (((1,), (1,)), ((), ())), preferred_element_type=jnp.float32
            )
            before = top[q, rows, :]
            after = jnp.maximum(before, jnp.max(scores, axis=1, keepdims=True))
            weights = jnp.exp2((scores - jnp.concatenate([after] * (KEYS // HD), axis=1)) * SCALE)
            factor = jnp.exp2((before - after) * SCALE)
            mixed = jnp.dot(weights.astype(jnp.bfloat16), vaug[...], preferred_element_type=jnp.float32)
            acc[q, rows, :] = acc[q, rows, :] * jnp.concatenate([factor] * 2, axis=1) + mixed
            top[q, rows, :] = after

        @pl.when(p == SLICES - 1)
        def _():
            done = (acc[q, :, :HD] / acc[q, :, HD:]).astype(jnp.bfloat16)
            for g in range(GROUP):
                o_out[q, :, pl.ds(g * HD, HD)] = done[g * HALF : (g + 1) * HALF]

        return 0

    lax.fori_loop(0, 4 * SLICES, unit, 0)
    send_out(1)

    for i in range(1, len(partners)):
        for which in range(3):
            inward(which, i).wait_send()
    for p in range(SLICES):
        for which in range(2):
            for way in ways(p) + [3]:
                hop(which, p, way).wait_send()
    for t in range(2):
        for dx in range(NX):
            local, remote = outward(dx, t)
            if dx:
                remote.wait_send()
            else:
                pl.when(ys != t)(remote.wait_send)
    for dx in range(NX):
        for s in range(2):
            pltpu.make_async_copy(
                o_out.at[pl.ds(0, 2), pl.ds(0, 16), :],
                out_ref.at[:, :, pl.ds(0, COLS)],
                out_recv.at[dx * 2 + s],
            ).wait()


def on_device(queries, keys, values, doc_ids):
    bf16, f32 = jnp.bfloat16, jnp.float32
    anywhere = pl.BlockSpec(memory_space=pl.ANY)
    pieces = pltpu.VMEM((SLICES, 4, 4, HALF, HD), bf16)
    return pl.pallas_call(
        kernel,
        out_shape=jax.ShapeDtypeStruct(queries.shape, bf16),
        in_specs=[pl.BlockSpec(memory_space=pltpu.SMEM), anywhere, anywhere, anywhere],
        out_specs=anywhere,
        scratch_shapes=[
            pieces,
            pieces,
            pltpu.VMEM((4, HALF, COLS), bf16),
            pltpu.VMEM((4, ROWS, 2 * HD), bf16),
            pltpu.VMEM((KEYS, 2 * HD), bf16),
            pltpu.VMEM((KEYS, 2 * HD), bf16),
            pltpu.VMEM((4, ROWS, 2 * HD), f32),
            pltpu.VMEM((4, ROWS, HD), f32),
            pltpu.VMEM((4, HALF, COLS), bf16),
            pltpu.SemaphoreType.DMA((3, 8)),
            pltpu.SemaphoreType.DMA((3, 8)),
            pltpu.SemaphoreType.DMA((2, SLICES, 5)),
            pltpu.SemaphoreType.DMA((2, SLICES, 4)),
            pltpu.SemaphoreType.DMA((8,)),
            pltpu.SemaphoreType.DMA((8,)),
        ],
        compiler_params=pltpu.CompilerParams(
            collective_id=0, has_side_effects=True, vmem_limit_bytes=40 * 1024 * 1024
        ),
        cost_estimate=pl.CostEstimate(
            flops=4 * ROWS * 4 * KEYS * SLICES * HD, bytes_accessed=2 * queries.size * 2, transcendentals=0
        ),
    )(doc_ids, queries, keys, values)


def solution(mesh):
    in_specs = (P("ctx", "head", None), P("ctx", "head", None), P("ctx", "head", None), P())
    out_specs = P("ctx", "head", None)
    return jax.shard_map(
        on_device, mesh=mesh, in_specs=in_specs, out_specs=out_specs, check_vma=False
    )
```

time: 408 us -> 111 us (0.27)
  the two profiles are of different devices: /device:TPU:224 before, /device:TPU:8 now
where the time goes in v1:
time: 111 us; the launch traced here: 110 us
  Pallas kernels  106 us (95%)
  local copies, waits for them, and re-layouts  4.17 us (4%)
    pallas_call x1, Pallas kernels, on_device(): pl.pallas_call(kernel, out_shape=jax.ShapeDtypeStruct(queries.shape, bf16...  106 us
    unnamed x9, local copies, waits for them, and re-layouts  4.17 us

profile of v1, /device:TPU:8, one launch (start us, length us, event | category | flops | bytes accessed | tf_op | source)
XLA Modules:
  0.0 110.5 jit_solution(17696102835287062251)
XLA Ops:
  0.0 0.0 copy-start
  0.0 1.0 copy-done
  1.0 0.0 copy-start.1
  1.0 0.8 copy-done.1
  1.9 0.0 copy-start.2
  1.9 0.8 copy-done.2
  2.7 0.0 copy-start.3
  2.7 0.7 copy-done.3
  3.4 106.3 %shard_map.46 = bf16[2,16,8192]{2,1,0:T(8,128)(2,1)S(1)} custom-call(s32[128]{0:T(128)S(1)} %copy-done.3, bf16[2,16,8192]{2,1,0:T(8,128)(2,1)S(1)} %copy-done, bf16[2,16,1024]{2,1,0:T(8,128)(2,1)S(1)} %copy-done.1, bf16[2,16,1024]{2,1,0:T(8,128)(2,1)S(1)} %copy-done.2), custom_call_target="tpu_custom_call" | custom-call | flops 10737418240 | bytes 1048576 | tf_op jit(solution)/shard_map/pallas_call | solution.py:298
  109.7 0.8 copy.6
Async XLA Ops:
  0.0 1.0 copy-start
  1.0 0.8 copy-start.1
  1.9 0.8 copy-start.2
  2.7 0.7 copy-start.3

commit v2 on v1

v2 whole, which is shorter than its diff:
```python
import jax
import jax.numpy as jnp
from jax import lax
from jax.experimental import pallas as pl
from jax.experimental.pallas import tpu as pltpu
from jax.sharding import PartitionSpec as P

HD = 128
GROUP = 8
BLK = 128
HALF = 64
COLS = GROUP * HD
NX, NZ, NLO = 4, 16, 8

BACK = (0, 1, 2, 3, 4, 4, 3, 2, 1, 0)
SLICES = len(BACK)
UP = {0: 1, 1: 2, 2: 3, 3: 5}
DOWN = {4: 6, 6: 7, 7: 8, 8: 9}
CROSS = ((1, 2, 3, 4, 5, 6, 7, 8), (0, 1, 2, 3, 6, 7, 8, 9))
UNITS = 9
HALF_KEYS = 8 * HALF
KEYS = 2 * HALF_KEYS
ROWS = GROUP * HALF
BIG = -1e30
SCALE = HD**-0.5 * 1.4426950408889634
MESH = pl.DeviceIdType.MESH
FAR_AT = {4: 1, 5: 3}
TRANSIT_AT, TURN_AT = 2, 6
FORWARD = {1: 2, 3: 3, 5: 4, 6: 5, 7: 6, 9: 7, 11: 8, 13: 9}


def kernel(
    doc_ref, q_ref, k_ref, v_ref, out_ref,
    kbuf, vbuf, transit, q_in, qaug, kaug, vaug, acc, top, o_out,
    in_send, in_recv, hop_send, hop_recv, transit_send, transit_recv, out_send, out_recv,
):
    head, ctx = lax.axis_index("head"), lax.axis_index("ctx")
    x, zhi = lax.rem(head, NX), lax.div(head, NX)
    lo, y, c = lax.div(ctx, 8), lax.rem(lax.div(ctx, 2), 4), lax.rem(ctx, 2)
    z = zhi * NLO + lo
    yh, ys = lax.div(y, 2), lax.rem(y, 2)

    def device(x, y, z, c):
        return (lax.div(z, NLO) * NX + x, lax.rem(z, NLO) * 8 + y * 2 + c)

    def turn(v, by, n):
        return lax.rem(v + by + n, n)

    def side(y):
        return lax.rem(lax.div(y + 1, 2), 2)

    y_pair = yh * 2 + 1 - ys
    y_same = 3 - y
    own, other = yh * 2 + c, (1 - yh) * 2 + c
    my_head = 2 * x + side(y)
    sibling = device(x, y, z, 1 - c)
    across = device(x, y_same, z, c)
    above = device(x, y, turn(z, 1, NZ), c)
    below = device(x, y, turn(z, -1, NZ), c)
    far_lo = jnp.minimum(lo + 4, NLO - 1)
    far = device(x, y, (1 - zhi) * NLO + far_lo, c)
    stop = device(x, y, (1 - zhi) * NLO + lax.rem(lo + 4, NLO), c)
    past_stop = device(x, y, zhi * NLO + lax.rem(lo + 4, NLO), c)
    rests, goes_up = (lo == 2) | (lo == 3), lo >= 6
    far_slot = jnp.where(lo < 4, 4, lo + 2)
    partners = [(dx, dy) for dx in range(NX) for dy in range(2)]
    to_above, to_below = lo < NLO - 1, lo > 0

    barrier = pltpu.get_barrier_semaphore()

    def greet(one):
        pl.semaphore_signal(barrier, inc=1, device_id=one, device_id_type=MESH)

    for dx, dy in partners[1:]:
        greet(device(turn(x, dx, NX), (y, y_pair)[dy], z, c))
    greet(sibling)
    greet(across)
    pl.when(to_above)(lambda: greet(above))
    pl.when(to_below)(lambda: greet(below))
    for source in range(6):
        pl.when(lo == min(source + 4, NLO - 1))(lambda: greet(device(x, y, (1 - zhi) * NLO + source, c)))
    pl.when(rests)(lambda: greet(stop))
    pl.when(goes_up)(lambda: greet(past_stop))
    count = to_above.astype(jnp.int32) + to_below.astype(jnp.int32) + rests.astype(jnp.int32)
    pl.semaphore_wait(barrier, 10 + count)

    here = pl.ds(pl.multiple_of(x * 16, 16), 16)

    def inward(which, i):
        dx, dy = partners[i]
        xd, yd = turn(x, dx, NX), (y, y_pair)[dy]
        h = 2 * xd + side(yd)
        if which == 2:
            src = q_ref.at[:, :, pl.ds(pl.multiple_of(h * COLS, COLS), COLS)]
            dst = q_in.at[pl.ds(ys * 2, 2), here, :]
        else:
            src = (k_ref, v_ref)[which].at[:, :, pl.ds(pl.multiple_of(h * HD, HD), HD)]
            dst = (kbuf, vbuf)[which].at[0, own, pl.ds(ys * 2, 2), here, :]
        if i == 0:
            return pltpu.make_async_copy(src, dst, in_recv.at[which, 0])
        return pltpu.make_async_remote_copy(
            src_ref=src, dst_ref=dst, send_sem=in_send.at[which, i], recv_sem=in_recv.at[which, i],
            device_id=device(xd, yd, z, c), device_id_type=MESH,
        )

    def arrived(which):
        for i in range(len(partners)):
            copy = inward(which, i)
            copy.wait() if i == 0 else copy.wait_recv()

    for which in range(3):
        for i in range(len(partners)):
            inward(which, i).start()

    def valid(p):
        back = jnp.int32(0)
        for at, by in enumerate(BACK):
            back = jnp.where(p == at, by, back)
        return lo >= back

    def hop(which, p, way):
        buf = (kbuf, vbuf)[which]
        src, dst_p, slot = own, p, 0
        if way == 0:
            dst_p, to = (UP[p], above) if p in UP else (DOWN[p], below) if p in DOWN else (8, above)
        elif way == 1:
            to, slot = across, 1
        elif way == 2:
            to, slot = sibling, 2
        elif way == 3:
            src, to, slot = other, sibling, 3
        else:
            dst_p, to = far_slot, far
        return pltpu.make_async_remote_copy(
            src_ref=buf.at[p, src], dst_ref=buf.at[dst_p, src],
            send_sem=hop_send.at[which, p, way], recv_sem=hop_recv.at[which, dst_p, slot],
            device_id=to, device_id_type=MESH,
        )

    def rest(which, leg):
        return pltpu.make_async_remote_copy(
            src_ref=transit.at[which] if leg else (kbuf, vbuf)[which].at[0, own],
            dst_ref=(kbuf, vbuf)[which].at[9, own] if leg else transit.at[which],
            send_sem=transit_send.at[which, leg],
            recv_sem=hop_recv.at[which, 9, 0] if leg else transit_recv.at[which],
            device_id=past_stop if leg else stop, device_id_type=MESH,
        )

    def landed(which, p, slot):
        buf = (kbuf, vbuf)[which]
        pltpu.make_async_remote_copy(
            src_ref=buf.at[p, own], dst_ref=buf.at[p, own],
            send_sem=hop_send.at[which, p, 1], recv_sem=hop_recv.at[which, p, slot],
            device_id=across, device_id_type=MESH,
        ).wait_recv()

    def sends(which, p, act, early=True):
        if p in UP:
            pl.when(to_above)(lambda: act(hop(which, p, 0)))
        elif p == 8:
            pl.when(lo < NLO - 1)(lambda: act(hop(which, p, 0)))
        elif p in DOWN:
            act(hop(which, p, 0))
        if p == 0 and early:
            pl.when(lo < 4)(lambda: act(hop(which, p, 4)))
            pl.when(goes_up)(lambda: act(rest(which, 0)))
        if p in (4, 5):
            pl.when(yh == 1)(lambda: act(hop(which, p, 1)))
        elif p in (0, 9):
            pl.when(yh == 0)(lambda: act(hop(which, p, 1)))
        else:
            act(hop(which, p, 1))
        act(hop(which, p, 2))

    def forward(p):
        @pl.when(valid(p))
        def _():
            for which in range(2):
                if p == 0:
                    arrived(which)
                elif p == 9:
                    pl.when(lo != 6)(lambda: landed(which, p, 0))
                else:
                    landed(which, p, 0)
                sends(which, p, lambda copy: copy.start())

    def crossed(m):
        p = jnp.int32(0)
        for at in range(len(CROSS[0])):
            p = jnp.where(m == at, jnp.where(yh == 0, CROSS[0][at], CROSS[1][at]), p)
        return p

    def cross(m):
        p = crossed(m)

        @pl.when(valid(p))
        def _():
            for which in range(2):
                landed(which, p, 1)
                hop(which, p, 3).start()

    def ready(p, slot):
        @pl.when(valid(p))
        def _():
            for which in range(2):
                landed(which, p, slot)

    lane = lax.broadcasted_iota(jnp.int32, (1, HD), 1)
    lanes = lax.broadcasted_iota(jnp.int32, (ROWS, HD), 1)
    ones = jnp.ones((HALF, HD), jnp.bfloat16)
    for q in range(4):
        qaug[q, :, HD:] = jnp.where(lanes == q, 1.0, 0.0).astype(jnp.bfloat16)
    vaug[:, HD:] = jnp.ones((KEYS, HD), jnp.bfloat16)

    forward(0)
    forward(1)
    arrived(2)
    for q in range(4):
        for g in range(GROUP):
            qaug[q, pl.ds(g * HALF, HALF), :HD] = q_in[q, :, pl.ds(g * HD, HD)]

    for q in range(4):
        block_keys = kbuf[0, own, q]
        block_values = jnp.concatenate([vbuf[0, own, q], ones], axis=1)
        scores = lax.dot_general(
            qaug[q, :, :HD], block_keys, (((1,), (1,)), ((), ())), preferred_element_type=jnp.float32
        )
        key = lax.broadcasted_iota(jnp.int32, (ROWS, HALF), 1)
        token = lax.rem(lax.broadcasted_iota(jnp.int32, (ROWS, HALF), 0), HALF)
        scores = jnp.where(key <= token, scores, BIG)
        best = jnp.max(scores, axis=1, keepdims=True)
        weights = jnp.exp2((scores - best) * SCALE)
        acc[q] = jnp.dot(weights.astype(jnp.bfloat16), block_values, preferred_element_type=jnp.float32)
        top[q] = jnp.broadcast_to(best, (ROWS, HD))

    query_blocks = [lo * 16 + (yh * 2 + q // 2) * 4 + c * 2 + q % 2 for q in range(4)]

    def prepare(p, half_of_y, at):
        there = valid(p)
        rows = pl.ds(at * HALF_KEYS, HALF_KEYS)

        @pl.when(there)
        def _():
            kaug[rows, :HD] = kbuf[p, pl.ds(half_of_y * 2, 2)].reshape(HALF_KEYS, HD)
            vaug[rows, :HD] = vbuf[p, pl.ds(half_of_y * 2, 2)].reshape(HALF_KEYS, HD)

        @pl.when(jnp.logical_not(there))
        def _():
            kaug[rows, :HD] = jnp.zeros((HALF_KEYS, HD), jnp.bfloat16)
            vaug[rows, :HD] = jnp.zeros((HALF_KEYS, HD), jnp.bfloat16)

        back = jnp.int32(0)
        for slot, by in enumerate(BACK):
            back = jnp.where(p == slot, by, back)
        alike = (p != 0) & (zhi == 1)
        docs = [doc_ref[b] for b in query_blocks]
        for i in range(8):
            block = (lo - back) * 16 + (half_of_y * 2 + i // 2 % 2) * 4 + i // 4 * 2 + i % 2
            doc = doc_ref[jnp.maximum(block, 0)]
            mask = jnp.zeros((1, HD), jnp.float32)
            for q in range(4):
                seen = (block < query_blocks[q]) | ((block == query_blocks[q]) & alike)
                seen = seen & (block >= 0) & (doc == docs[q])
                mask = jnp.where(lane == q, jnp.where(seen, 0.0, BIG), mask)
            tile = pl.ds(at * HALF_KEYS + i * HALF, HALF)
            kaug[tile, HD:] = jnp.broadcast_to(mask, (HALF, HD)).astype(jnp.bfloat16)

    def outward(dx, t):
        xd, yd = turn(x, dx, NX), yh * 2 + t
        src = o_out.at[pl.ds(t * 2, 2), pl.ds(pl.multiple_of(xd * 16, 16), 16), :]
        dst = out_ref.at[:, :, pl.ds(pl.multiple_of(my_head * COLS, COLS), COLS)]
        sem = out_recv.at[dx * 2 + ys]
        local = pltpu.make_async_copy(src, dst, sem)
        remote = pltpu.make_async_remote_copy(
            src_ref=src, dst_ref=dst, send_sem=out_send.at[dx * 2 + t], recv_sem=sem,
            device_id=device(xd, yd, z, c), device_id_type=MESH,
        )
        return local, remote

    def send_out(t):
        for dx in (2, 1, 3, 0):
            local, remote = outward(dx, t)
            if dx:
                remote.start()
            else:
                pl.when(ys == t)(local.start)
                pl.when(ys != t)(remote.start)

    def send_far(source):
        @pl.when(lo == source)
        def _():
            for which in range(2):
                hop(which, 0, 4).start()

    def pass_on():
        @pl.when(rests)
        def _():
            for which in range(2):
                rest(which, 0).wait_recv()
                rest(which, 1).start()

    def turn_up():
        @pl.when(lo == 6)
        def _():
            for which in range(2):
                landed(which, 9, 0)
                hop(which, 9, 0).start()

    events = {TRANSIT_AT: [pass_on], TURN_AT: [turn_up]}
    for source, u in FAR_AT.items():
        events.setdefault(u, []).append(lambda source=source: send_far(source))
    for u, p in FORWARD.items():
        events.setdefault(u, []).append(lambda p=p: forward(p))
    for m in range(len(CROSS[0])):
        events.setdefault(2 * m + 1, []).append(lambda m=m: cross(m))
        events.setdefault(2 * m + 2, []).append(lambda m=m: ready(crossed(m), 3))
    for p in range(SLICES):
        events.setdefault(max(0, 2 * (p - 1)), []).append(lambda p=p: ready(p, 2))
    events.setdefault(2 * UNITS - 1, []).append(lambda: send_out(0))

    def half_unit(u, _):
        i, h = lax.div(u, 2), lax.rem(u, 2)
        for when, what in sorted(events.items()):

            @pl.when(u == when)
            def _(what=what):
                for act in what:
                    act()

        first = jnp.where(i == 0, 0, crossed(i - 1))
        second = i + 1

        @pl.when(valid(first) | valid(second))
        def _():
            @pl.when(h == 0)
            def _():
                prepare(first, jnp.where(i == 0, yh, 1 - yh), 0)
                prepare(second, yh, 1)

            def scores_of(q):
                return lax.dot_general(
                    qaug[q], kaug[...], (((1,), (1,)), ((), ())), preferred_element_type=jnp.float32
                )

            def soften(q, scores):
                before = top[q]
                after = jnp.maximum(before, jnp.max(scores, axis=1, keepdims=True))
                top[q] = after
                weights = jnp.exp2((scores - jnp.concatenate([after] * (KEYS // HD), axis=1)) * SCALE)
                return weights.astype(jnp.bfloat16), jnp.exp2((before - after) * SCALE)

            def mix(q, weights, factor):
                mixed = jnp.dot(weights, vaug[...], preferred_element_type=jnp.float32)
                acc[q] = acc[q] * jnp.concatenate([factor] * 2, axis=1) + mixed

            q = h * 2
            scores = scores_of(q)
            later_scores = scores_of(q + 1)
            weights, factor = soften(q, scores)
            later = soften(q + 1, later_scores)
            mix(q, weights, factor)
            mix(q + 1, *later)

        @pl.when(i == UNITS - 1)
        def _():
            for j in range(2):
                q = h * 2 + j
                done = (acc[q, :, :HD] / acc[q, :, HD:]).astype(jnp.bfloat16)
                for g in range(GROUP):
                    o_out[q, :, pl.ds(g * HD, HD)] = done[g * HALF : (g + 1) * HALF]

        return 0

    lax.fori_loop(0, 2 * UNITS, half_unit, 0)
    send_out(1)

    for i in range(1, len(partners)):
        for which in range(3):
            inward(which, i).wait_send()
    for p in range(SLICES):

        @pl.when(valid(p))
        def _(p=p):
            for which in range(2):
                sends(which, p, lambda copy: copy.wait_send(), False)
                if p == 0:
                    pl.when(lo < 6)(lambda: hop(which, 0, 4).wait_send())
                    pl.when(goes_up)(lambda: rest(which, 0).wait_send())
                if p == 9:
                    pl.when(rests)(lambda: rest(which, 1).wait_send())
                    pl.when(lo == 6)(lambda: hop(which, 9, 0).wait_send())

    for m in range(len(CROSS[0])):
        p = crossed(m)

        @pl.when(valid(p))
        def _(p=p):
            for which in range(2):
                hop(which, p, 3).wait_send()

    for t in range(2):
        for dx in range(NX):
            local, remote = outward(dx, t)
            if dx:
                remote.wait_send()
            else:
                pl.when(ys != t)(remote.wait_send)
    for dx in range(NX):
        for s in range(2):
            pltpu.make_async_copy(
                o_out.at[pl.ds(0, 2), pl.ds(0, 16), :],
                out_ref.at[:, :, pl.ds(0, COLS)],
                out_recv.at[dx * 2 + s],
            ).wait()


def on_device(queries, keys, values, doc_ids):
    bf16, f32 = jnp.bfloat16, jnp.float32
    anywhere = pl.BlockSpec(memory_space=pl.ANY)
    pieces = pltpu.VMEM((SLICES, 4, 4, HALF, HD), bf16)
    return pl.pallas_call(
        kernel,
        out_shape=jax.ShapeDtypeStruct(queries.shape, bf16),
        in_specs=[pl.BlockSpec(memory_space=pltpu.SMEM)] + [pl.BlockSpec(memory_space=pltpu.HBM)] * 3,
        out_specs=anywhere,
        scratch_shapes=[
            pieces,
            pieces,
            pltpu.VMEM((2, 4, HALF, HD), bf16),
            pltpu.VMEM((4, HALF, COLS), bf16),
            pltpu.VMEM((4, ROWS, 2 * HD), bf16),
            pltpu.VMEM((KEYS, 2 * HD), bf16),
            pltpu.VMEM((KEYS, 2 * HD), bf16),
            pltpu.VMEM((4, ROWS, 2 * HD), f32),
            pltpu.VMEM((4, ROWS, HD), f32),
            pltpu.VMEM((4, HALF, COLS), bf16),
            pltpu.SemaphoreType.DMA((3, 8)),
            pltpu.SemaphoreType.DMA((3, 8)),
            pltpu.SemaphoreType.DMA((2, SLICES, 5)),
            pltpu.SemaphoreType.DMA((2, SLICES, 4)),
            pltpu.SemaphoreType.DMA((2, 2)),
            pltpu.SemaphoreType.DMA((2,)),
            pltpu.SemaphoreType.DMA((8,)),
            pltpu.SemaphoreType.DMA((8,)),
        ],
        compiler_params=pltpu.CompilerParams(
            collective_id=0, has_side_effects=True, vmem_limit_bytes=62 * 1024 * 1024
        ),
        cost_estimate=pl.CostEstimate(
            flops=4 * ROWS * 4 * KEYS * UNITS * HD, bytes_accessed=2 * queries.size * 2, transcendentals=0
        ),
    )(doc_ids, queries, keys, values)


def solution(mesh):
    in_specs = (P("ctx", "head", None), P("ctx", "head", None), P("ctx", "head", None), P())
    out_specs = P("ctx", "head", None)
    return jax.shard_map(
        on_device, mesh=mesh, in_specs=in_specs, out_specs=out_specs, check_vma=False
    )
```

time: 111 us -> 76.4 us (0.69)
  the two profiles are of different devices: /device:TPU:8 before, /device:TPU:88 now
where the time goes in v2:
time: 76.4 us; the launch traced here: 76.2 us
  Pallas kernels  74.3 us (97%)
  local copies, waits for them, and re-layouts  1.87 us (2%)
    pallas_call x1, Pallas kernels, on_device(): pl.pallas_call(kernel, out_shape=jax.ShapeDtypeStruct(queries.shape, bf16...  74.3 us
    unnamed x1, local copies, waits for them, and re-layouts  1.87 us

profile of v2, /device:TPU:88, one launch (start us, length us, event | category | flops | bytes accessed | tf_op | source)
XLA Modules:
  0.0 76.2 jit_solution(11361408556513711990)
XLA Ops:
  0.0 74.3 %shard_map.46 = bf16[2,16,8192]{2,1,0:T(8,128)(2,1)} custom-call(s32[128]{0:T(128)} %doc_ref.1, bf16[2,16,8192]{2,1,0:T(8,128)(2,1)} %q_ref.1, bf16[2,16,1024]{2,1,0:T(8,128)(2,1)} %k_ref.1, bf16[2,16,1024]{2,1,0:T(8,128)(2,1)} %v_ref.1), custom_call_target="tpu_custom_call" | custom-call | flops 9663676416 | bytes 1048576 | tf_op jit(solution)/shard_map/pallas_call | solution.py:421
  74.3 1.9 %copy.6 = bf16[2,16,8192]{2,1,0:T(8,128)(2,1)} copy(bf16[2,16,8192]{2,1,0:T(8,128)(2,1)} %shard_map.46) | data formatting | bytes 1048576

commit v3 on v2

v3 whole, which is shorter than its diff:
```python
import jax
import jax.numpy as jnp
from jax import lax
from jax.experimental import pallas as pl
from jax.experimental.pallas import tpu as pltpu
from jax.sharding import PartitionSpec as P

HD = 128
GROUP = 8
BLK = 128
HALF = 64
COLS = GROUP * HD
NX, NZ, NLO = 4, 16, 8

SLICES = 10
UNITS = 9
HALF_KEYS = 8 * HALF
KEYS = 2 * HALF_KEYS
ROWS = GROUP * HALF
BIG = -1e30
SCALE = HD**-0.5 * 1.4426950408889634
MESH = pl.DeviceIdType.MESH
FAR_AT = {4: 1, 5: 2}
TRANSIT_AT, TURN_AT = 5, 8


def back_of(p):
    return jnp.minimum(jnp.minimum(p, 4), SLICES - 1 - p)


def onward_of(p):
    return p + 1 + ((p == 3) | (p == 4)).astype(jnp.int32)


def kernel(
    doc_ref, q_ref, k_ref, v_ref, out_ref,
    kv, transit, q_in, qaug, kaug, vaug, acc, top, o_out,
    in_send, in_recv, hop_send, hop_recv, transit_send, transit_recv, out_send, out_recv, ack,
):
    head, ctx = lax.axis_index("head"), lax.axis_index("ctx")
    x, zhi = lax.rem(head, NX), lax.div(head, NX)
    lo, y, c = lax.div(ctx, 8), lax.rem(lax.div(ctx, 2), 4), lax.rem(ctx, 2)
    z = zhi * NLO + lo
    yh, ys = lax.div(y, 2), lax.rem(y, 2)

    def device(x, y, z, c):
        return (lax.div(z, NLO) * NX + x, lax.rem(z, NLO) * 8 + y * 2 + c)

    def turn(v, by, n):
        return lax.rem(v + by + n, n)

    def side(y):
        return lax.rem(lax.div(y + 1, 2), 2)

    y_pair = yh * 2 + 1 - ys
    y_same = 3 - y
    own, other = yh * 2 + c, (1 - yh) * 2 + c
    my_head = 2 * x + side(y)
    sibling = device(x, y, z, 1 - c)
    across = device(x, y_same, z, c)
    above = device(x, y, turn(z, 1, NZ), c)
    below = device(x, y, turn(z, -1, NZ), c)
    far_lo = jnp.minimum(lo + 4, NLO - 1)
    far = device(x, y, (1 - zhi) * NLO + far_lo, c)
    stop = device(x, y, (1 - zhi) * NLO + lax.rem(lo + 4, NLO), c)
    past_stop = device(x, y, zhi * NLO + lax.rem(lo + 4, NLO), c)
    rests, goes_up = (lo == 2) | (lo == 3), lo >= 6
    far_slot = jnp.where(lo < 4, 4, lo + 2)
    partners = [(dx, dy) for dx in range(NX) for dy in range(2)]
    to_above, to_below = lo < NLO - 1, lo > 0

    barrier = pltpu.get_barrier_semaphore()

    def greet(one):
        pl.semaphore_signal(barrier, inc=1, device_id=one, device_id_type=MESH)

    for dx, dy in partners[1:]:
        greet(device(turn(x, dx, NX), (y, y_pair)[dy], z, c))
    greet(sibling)
    greet(across)
    pl.when(to_above)(lambda: greet(above))
    pl.when(to_below)(lambda: greet(below))
    pl.when(goes_up)(lambda: greet(past_stop))

    def from_other_half(tell):
        for source in range(6):
            pl.when(lo == min(source + 4, NLO - 1))(lambda: tell(device(x, y, (1 - zhi) * NLO + source, c)))
        pl.when(rests)(lambda: tell(stop))

    pl.when(zhi == 0)(lambda: from_other_half(greet))
    pl.when((zhi == 0) & (lo < 6))(lambda: greet(far))
    pl.when((zhi == 0) & goes_up)(lambda: greet(stop))
    welcomed = jnp.where(lo == NLO - 1, 3, jnp.where(lo >= 2, 1, 0))
    count = to_above.astype(jnp.int32) + to_below.astype(jnp.int32) + rests.astype(jnp.int32)
    pl.semaphore_wait(barrier, 9 + zhi * (1 + welcomed) + count)

    def welcome(one):
        pl.semaphore_signal(ack, inc=1, device_id=one, device_id_type=MESH)

    pl.when(zhi == 1)(lambda: from_other_half(welcome))

    here = pl.ds(pl.multiple_of(x * 16, 16), 16)

    def inward(which, i):
        xd, yd = turn(x, lax.div(i, 2), NX), jnp.where(lax.rem(i, 2) == 0, y, y_pair)
        h = 2 * xd + side(yd)
        if which == 2:
            src = q_ref.at[:, :, pl.ds(pl.multiple_of(h * COLS, COLS), COLS)]
            dst = q_in.at[pl.ds(ys * 2, 2), here, :]
        else:
            src = (k_ref, v_ref)[which].at[:, :, pl.ds(pl.multiple_of(h * HD, HD), HD)]
            dst = kv.at[which, 0, own, pl.ds(ys * 2, 2), here, :]
        local = pltpu.make_async_copy(src, dst, in_recv.at[which, 0])
        remote = pltpu.make_async_remote_copy(
            src_ref=src, dst_ref=dst, send_sem=in_send.at[which, i], recv_sem=in_recv.at[which, i],
            device_id=device(xd, yd, z, c), device_id_type=MESH,
        )
        return local, remote

    def each(first, last, act):
        def step(i, _):
            act(i)
            return 0

        lax.fori_loop(first, last, step, 0)

    def arrived(which):
        inward(which, jnp.int32(0))[0].wait()
        each(1, 2 * NX, lambda i: inward(which, i)[1].wait_recv())

    for which in range(3):
        inward(which, jnp.int32(0))[0].start()
        each(1, 2 * NX, lambda i: inward(which, i)[1].start())

    def valid(p):
        return lo >= back_of(p)

    def hop(which, p, way):
        src, dst_p, slot = own, p, 0
        if way == 0:
            dst_p, to = onward_of(p), device(x, y, turn(z, jnp.where(p < 4, 1, -1), NZ), c)
        elif way == 1:
            to, slot = across, 1
        elif way == 2:
            to, slot = sibling, 2
        elif way == 3:
            src, to, slot = other, sibling, 3
        elif way == 4:
            dst_p, to = far_slot, far
        else:
            dst_p, to = 8, above
        return pltpu.make_async_remote_copy(
            src_ref=kv.at[which, p, src], dst_ref=kv.at[which, dst_p, src],
            send_sem=hop_send.at[which, p, way], recv_sem=hop_recv.at[which, dst_p, slot],
            device_id=to, device_id_type=MESH,
        )

    def rest(which, leg):
        return pltpu.make_async_remote_copy(
            src_ref=transit.at[which] if leg else kv.at[which, 0, own],
            dst_ref=kv.at[which, 9, own] if leg else transit.at[which],
            send_sem=transit_send.at[which, leg],
            recv_sem=hop_recv.at[which, 9, 0] if leg else transit_recv.at[which],
            device_id=past_stop if leg else stop, device_id_type=MESH,
        )

    def landed(which, p, slot):
        pltpu.make_async_remote_copy(
            src_ref=kv.at[which, p, own], dst_ref=kv.at[which, p, own],
            send_sem=hop_send.at[which, p, 1], recv_sem=hop_recv.at[which, p, slot],
            device_id=across, device_id_type=MESH,
        ).wait_recv()

    def sends(which, p, act):
        up, down = (p < 4) & to_above, (p == 4) | (p == 6) | (p == 7) | ((p == 8) & (lo < NLO - 1))
        pl.when(up | down)(lambda: act(hop(which, p, 0)))
        to_upper, to_lower = (p != 4) & (p != 5), (p != 0) & (p != 9)
        pl.when(((yh == 0) & to_upper) | ((yh == 1) & to_lower))(lambda: act(hop(which, p, 1)))
        act(hop(which, p, 2))

    def forward(which, p):
        @pl.when(valid(p))
        def _():
            pl.when((p != 9) | (lo != 6))(lambda: landed(which, p, 0))
            sends(which, p, lambda copy: copy.start())

    def crossed(m):
        return jnp.where(yh == 0, m + 1, jnp.where(m < 4, m, m + 2))

    def cross(which, m):
        p = crossed(m)

        @pl.when(valid(p))
        def _():
            landed(which, p, 1)
            hop(which, p, 3).start()

    def ready(p, slot):
        @pl.when(valid(p))
        def _():
            for which in range(2):
                landed(which, p, slot)

    lane = lax.broadcasted_iota(jnp.int32, (1, HD), 1)
    lanes = lax.broadcasted_iota(jnp.int32, (ROWS, HD), 1)
    ones = jnp.ones((HALF, HD), jnp.bfloat16)

    def mark(q):
        qaug[q, :, HD:] = jnp.where(lanes == q, 1.0, 0.0).astype(jnp.bfloat16)

    each(0, 4, mark)

    def fill(i):
        vaug[pl.ds(pl.multiple_of(i * HALF, HALF), HALF), HD:] = ones

    each(0, KEYS // HALF, fill)

    for which in range(2):
        arrived(which)
        sends(which, jnp.int32(0), lambda copy: copy.start())
        pl.when((zhi == 1) & (lo < 4))(lambda: hop(which, 0, 4).start())
        pl.when((zhi == 1) & goes_up)(lambda: rest(which, 0).start())
    each(0, 2, lambda which: forward(which, jnp.int32(1)))
    arrived(2)

    def begin(q):
        for g in range(GROUP):
            qaug[q, pl.ds(g * HALF, HALF), :HD] = q_in[q, :, pl.ds(g * HD, HD)]
        block_values = jnp.concatenate([kv[1, 0, own, q], ones], axis=1)
        scores = lax.dot_general(
            qaug[q, :, :HD], kv[0, 0, own, q], (((1,), (1,)), ((), ())), preferred_element_type=jnp.float32
        )
        key = lax.broadcasted_iota(jnp.int32, (ROWS, HALF), 1)
        token = lax.rem(lax.broadcasted_iota(jnp.int32, (ROWS, HALF), 0), HALF)
        scores = jnp.where(key <= token, scores, BIG)
        best = jnp.max(scores, axis=1, keepdims=True)
        weights = jnp.exp2((scores - best) * SCALE)
        acc[q] = jnp.dot(weights.astype(jnp.bfloat16), block_values, preferred_element_type=jnp.float32)
        top[q] = jnp.broadcast_to(best, (ROWS, HD))

    each(0, 4, begin)

    query_blocks = [lo * 16 + (yh * 2 + q // 2) * 4 + c * 2 + q % 2 for q in range(4)]

    def prepare(p, half_of_y, at):
        there = valid(p)
        rows = pl.ds(pl.multiple_of(at * HALF_KEYS, HALF_KEYS), HALF_KEYS)

        @pl.when(there)
        def _():
            kaug[rows, :HD] = kv[0, p, pl.ds(half_of_y * 2, 2)].reshape(HALF_KEYS, HD)
            vaug[rows, :HD] = kv[1, p, pl.ds(half_of_y * 2, 2)].reshape(HALF_KEYS, HD)

        @pl.when(jnp.logical_not(there))
        def _():
            kaug[rows, :HD] = jnp.zeros((HALF_KEYS, HD), jnp.bfloat16)
            vaug[rows, :HD] = jnp.zeros((HALF_KEYS, HD), jnp.bfloat16)

        back = back_of(p)
        alike = (p != 0) & (zhi == 1)
        docs = [doc_ref[b] for b in query_blocks]
        for i in range(8):
            block = (lo - back) * 16 + (half_of_y * 2 + i // 2 % 2) * 4 + i // 4 * 2 + i % 2
            doc = doc_ref[jnp.maximum(block, 0)]
            mask = jnp.zeros((1, HD), jnp.float32)
            for q in range(4):
                seen = (block < query_blocks[q]) | ((block == query_blocks[q]) & alike)
                seen = seen & (block >= 0) & (doc == docs[q])
                mask = jnp.where(lane == q, jnp.where(seen, 0.0, BIG), mask)
            tile = pl.ds(pl.multiple_of(at * HALF_KEYS + i * HALF, HALF), HALF)
            kaug[tile, HD:] = jnp.broadcast_to(mask, (HALF, HD)).astype(jnp.bfloat16)

    def outward(dx, t):
        xd, yd = turn(x, dx, NX), yh * 2 + t
        src = o_out.at[pl.ds(t * 2, 2), pl.ds(pl.multiple_of(xd * 16, 16), 16), :]
        dst = out_ref.at[:, :, pl.ds(pl.multiple_of(my_head * COLS, COLS), COLS)]
        sem = out_recv.at[dx * 2 + ys]
        local = pltpu.make_async_copy(src, dst, sem)
        remote = pltpu.make_async_remote_copy(
            src_ref=src, dst_ref=dst, send_sem=out_send.at[dx * 2 + t], recv_sem=sem,
            device_id=device(xd, yd, z, c), device_id_type=MESH,
        )
        return local, remote

    def send_out(t):
        for dx in (2, 1, 3, 0):
            local, remote = outward(dx, t)
            if dx:
                remote.start()
            else:
                pl.when(ys == t)(local.start)
                pl.when(ys != t)(remote.start)

    def send_far():
        pl.when(zhi == 0)(lambda: pl.semaphore_wait(ack, 1))
        for which in range(2):
            hop(which, 0, 4).start()

    def set_out():
        @pl.when((zhi == 0) & ((lo < 4) | goes_up))
        def _():
            pl.semaphore_wait(ack, 1)
            for which in range(2):
                pl.when(lo < 4)(lambda: hop(which, 0, 4).start())
                pl.when(goes_up)(lambda: rest(which, 0).start())

    def pass_on():
        @pl.when(rests)
        def _():
            for which in range(2):
                rest(which, 0).wait_recv()
                rest(which, 1).start()

    def turn_up():
        @pl.when(lo == 6)
        def _():
            for which in range(2):
                landed(which, 9, 0)
                hop(which, 9, 5).start()

    ready(jnp.int32(0), 2)
    ready(jnp.int32(1), 2)

    def half_unit(u, _):
        i, h = lax.div(u, 2), lax.rem(u, 2)
        pl.when(u == 0)(set_out)
        pl.when(u == TRANSIT_AT)(pass_on)
        pl.when(u == TURN_AT)(turn_up)
        far_at = jnp.where(lo == 4, FAR_AT[4], jnp.where(lo == 5, FAR_AT[5], -1))
        pl.when(u == far_at)(send_far)
        pl.when(i < 7)(lambda: forward(h, i + 2 + (i > 2).astype(jnp.int32)))
        pl.when((u == 5) | (u == 6))(lambda: forward(1 - h, jnp.int32(5)))
        pl.when(i < UNITS - 1)(lambda: cross(h, i))

        @pl.when((h == 0) & (i > 0))
        def _():
            ready(crossed(i - 1), 3)
            ready(i + 1, 2)

        first = jnp.where(i == 0, 0, crossed(i - 1))
        second = i + 1

        @pl.when(valid(first) | valid(second))
        def _():
            @pl.when(h == 0)
            def _():
                def side_by_side(at):
                    near = (at == 1) | (i == 0)
                    prepare(jnp.where(at == 0, first, second), jnp.where(near, yh, 1 - yh), at)

                each(0, 2, side_by_side)

            def scores_of(q):
                return lax.dot_general(
                    qaug[q], kaug[...], (((1,), (1,)), ((), ())), preferred_element_type=jnp.float32
                )

            def soften(q, scores):
                before = top[q]
                after = jnp.maximum(before, jnp.max(scores, axis=1, keepdims=True))
                top[q] = after
                weights = jnp.exp2((scores - jnp.concatenate([after] * (KEYS // HD), axis=1)) * SCALE)
                return weights.astype(jnp.bfloat16), jnp.exp2((before - after) * SCALE)

            def mix(q, weights, factor):
                mixed = jnp.dot(weights, vaug[...], preferred_element_type=jnp.float32)
                acc[q] = acc[q] * jnp.concatenate([factor] * 2, axis=1) + mixed

            q = h * 2
            scores = scores_of(q)
            later_scores = scores_of(q + 1)
            weights, factor = soften(q, scores)
            later = soften(q + 1, later_scores)
            mix(q, weights, factor)
            mix(q + 1, *later)

        @pl.when(i == UNITS - 1)
        def _():
            def finish(j):
                q = h * 2 + j
                done = (acc[q, :, :HD] / acc[q, :, HD:]).astype(jnp.bfloat16)
                for g in range(GROUP):
                    o_out[q, :, pl.ds(g * HD, HD)] = done[g * HALF : (g + 1) * HALF]

            each(0, 2, finish)
            send_out(h)

        return 0

    lax.fori_loop(0, 2 * UNITS, half_unit, 0)

    def sent(i):
        for which in range(3):
            inward(which, i)[1].wait_send()

    each(1, 2 * NX, sent)

    def sent_on(p):
        @pl.when(valid(p))
        def _():
            for which in range(2):
                sends(which, p, lambda copy: copy.wait_send())

    each(0, SLICES, sent_on)

    def sent_across(m):
        p = crossed(m)

        @pl.when(valid(p))
        def _():
            for which in range(2):
                hop(which, p, 3).wait_send()

    each(0, UNITS - 1, sent_across)
    for which in range(2):
        pl.when(lo < 6)(lambda: hop(which, 0, 4).wait_send())
        pl.when(goes_up)(lambda: rest(which, 0).wait_send())
        pl.when(rests)(lambda: rest(which, 1).wait_send())
        pl.when(lo == 6)(lambda: hop(which, 9, 5).wait_send())
    for t in range(2):
        for dx in range(NX):
            local, remote = outward(dx, t)
            if dx:
                remote.wait_send()
            else:
                pl.when(ys != t)(remote.wait_send)
    for dx in range(NX):
        for s in range(2):
            pltpu.make_async_copy(
                o_out.at[pl.ds(0, 2), pl.ds(0, 16), :],
                out_ref.at[:, :, pl.ds(0, COLS)],
                out_recv.at[dx * 2 + s],
            ).wait()


def on_device(queries, keys, values, doc_ids):
    bf16, f32 = jnp.bfloat16, jnp.float32
    anywhere = pl.BlockSpec(memory_space=pl.ANY)
    return pl.pallas_call(
        kernel,
        out_shape=jax.ShapeDtypeStruct(queries.shape, bf16),
        in_specs=[pl.BlockSpec(memory_space=pltpu.SMEM)] + [pl.BlockSpec(memory_space=pltpu.HBM)] * 3,
        out_specs=anywhere,
        scratch_shapes=[
            pltpu.VMEM((2, SLICES, 4, 4, HALF, HD), bf16),
            pltpu.VMEM((2, 4, HALF, HD), bf16),
            pltpu.VMEM((4, HALF, COLS), bf16),
            pltpu.VMEM((4, ROWS, 2 * HD), bf16),
            pltpu.VMEM((KEYS, 2 * HD), bf16),
            pltpu.VMEM((KEYS, 2 * HD), bf16),
            pltpu.VMEM((4, ROWS, 2 * HD), f32),
            pltpu.VMEM((4, ROWS, HD), f32),
            pltpu.VMEM((4, HALF, COLS), bf16),
            pltpu.SemaphoreType.DMA((3, 8)),
            pltpu.SemaphoreType.DMA((3, 8)),
            pltpu.SemaphoreType.DMA((2, SLICES, 6)),
            pltpu.SemaphoreType.DMA((2, SLICES, 4)),
            pltpu.SemaphoreType.DMA((2, 2)),
            pltpu.SemaphoreType.DMA((2,)),
            pltpu.SemaphoreType.DMA((8,)),
            pltpu.SemaphoreType.DMA((8,)),
            pltpu.SemaphoreType.REGULAR,
        ],
        compiler_params=pltpu.CompilerParams(
            collective_id=0, has_side_effects=True, vmem_limit_bytes=62 * 1024 * 1024
        ),
        cost_estimate=pl.CostEstimate(
            flops=4 * ROWS * 4 * KEYS * UNITS * HD, bytes_accessed=2 * queries.size * 2, transcendentals=0
        ),
    )(doc_ids, queries, keys, values)


def solution(mesh):
    in_specs = (P("ctx", "head", None), P("ctx", "head", None), P("ctx", "head", None), P())
    out_specs = P("ctx", "head", None)
    return jax.shard_map(
        on_device, mesh=mesh, in_specs=in_specs, out_specs=out_specs, check_vma=False
    )
```

time: 76.4 us -> 70.1 us (0.918)
  the two profiles are of different devices: /device:TPU:88 before, /device:TPU:72 now
where the time goes in v3:
time: 70.1 us; the launch traced here: 69.9 us
  Pallas kernels  68 us (97%)
  local copies, waits for them, and re-layouts  1.87 us (3%)
    pallas_call x1, Pallas kernels, on_device(): pl.pallas_call(kernel, out_shape=jax.ShapeDtypeStruct(queries.shape, bf16...  68 us
    unnamed x1, local copies, waits for them, and re-layouts  1.87 us

profile of v3, /device:TPU:72, one launch (start us, length us, event | category | flops | bytes accessed | tf_op | source)
XLA Modules:
  0.0 69.9 jit_solution(7284504306436589726)
XLA Ops:
  0.0 68.0 %shard_map.46 = bf16[2,16,8192]{2,1,0:T(8,128)(2,1)} custom-call(s32[128]{0:T(128)} %doc_ref.1, bf16[2,16,8192]{2,1,0:T(8,128)(2,1)} %q_ref.1, bf16[2,16,1024]{2,1,0:T(8,128)(2,1)} %k_ref.1, bf16[2,16,1024]{2,1,0:T(8,128)(2,1)} %v_ref.1), custom_call_target="tpu_custom_call" | custom-call | flops 9663676416 | bytes 1048576 | tf_op jit(solution)/shard_map/pallas_call | solution.py:439
  68.0 1.9 %copy.6 = bf16[2,16,8192]{2,1,0:T(8,128)(2,1)} copy(bf16[2,16,8192]{2,1,0:T(8,128)(2,1)} %shard_map.46) | data formatting | bytes 1048576

commit v4 on v3

--- a/solution.py
+++ b/solution.py
@@ -129,8 +129,8 @@
         each(1, 2 * NX, lambda i: inward(which, i)[1].wait_recv())
 
     for which in range(3):
+        each(0, 2 * NX - 1, lambda k: inward(which, lax.rem(k + 3, 2 * NX - 1) + 1)[1].start())
         inward(which, jnp.int32(0))[0].start()
-        each(1, 2 * NX, lambda i: inward(which, i)[1].start())
 
     def valid(p):
         return lo >= back_of(p)

time: 70.1 us -> 69.9 us (level)
  no operation moved by 1% of the time
where the time goes in v4:
time: 69.9 us; the launch traced here: 69.7 us
  Pallas kernels  67.9 us (97%)
  local copies, waits for them, and re-layouts  1.87 us (3%)
    pallas_call x1, Pallas kernels, on_device(): pl.pallas_call(kernel, out_shape=jax.ShapeDtypeStruct(queries.shape, bf16...  67.9 us
    unnamed x1, local copies, waits for them, and re-layouts  1.87 us

profile of v4, /device:TPU:72, one launch (start us, length us, event | category | flops | bytes accessed | tf_op | source)
XLA Modules:
  0.0 69.7 jit_solution(15510324528490260661)
XLA Ops:
  0.0 67.9 %shard_map.46 = bf16[2,16,8192]{2,1,0:T(8,128)(2,1)} custom-call(s32[128]{0:T(128)} %doc_ref.1, bf16[2,16,8192]{2,1,0:T(8,128)(2,1)} %q_ref.1, bf16[2,16,1024]{2,1,0:T(8,128)(2,1)} %k_ref.1, bf16[2,16,1024]{2,1,0:T(8,128)(2,1)} %v_ref.1), custom_call_target="tpu_custom_call" | custom-call | flops 9663676416 | bytes 1048576 | tf_op jit(solution)/shard_map/pallas_call | solution.py:439
  67.9 1.9 %copy.6 = bf16[2,16,8192]{2,1,0:T(8,128)(2,1)} copy(bf16[2,16,8192]{2,1,0:T(8,128)(2,1)} %shard_map.46) | data formatting | bytes 1048576
